TPU v7x, 512 devices: a whole 4x4x16 slice. The times are simulated.
512 devices in a mesh: row: 16 (over x_hi, y, core), col: 32 (over x_lo, z).
Axes of the slice: x: 4 (x_hi: 2, x_lo: 2; x = x_hi * 2 + x_lo), y: 4, z: 16, core: 2. Of those that a mesh axis runs over, the one named last changes fastest.
Arguments:
- activations: bfloat16 [1024, 14848], P('col', 'row'), may hold values from -0.29882812 to 0.29882812
- out_grad: bfloat16 [1024, 29696], P('row', 'col'), may hold values from -4.1875 to 4.1875
- weight: bfloat16 [14848, 29696], P('row', 'col'), may hold values from -0.046875 to 0.046875
Outputs:
- d_input: bfloat16 [1024, 14848], P('col', 'row')
- d_weight: bfloat16 [14848, 29696], P('row', 'col')
All inputs are finite; a program needn't handle non-finite values.
Results may differ from a plain program's by a relative error of at most 0.001.
Values may be sent and summed in bfloat16 or wider, within the bound.
A program may use at most 64 MiB of HBM per device.

v0:
```python
import jax
import jax.numpy as jnp
from jax import lax
from jax.sharding import PartitionSpec as P


def outer_block(left, right):
    return lax.dot_general(
        left, right, (((0,), (0,)), ((), ())), preferred_element_type=jnp.float32
    )


def on_device(activations, out_grad, weight):
    grad_all = lax.all_gather(out_grad, "row", axis=0, tiled=True)
    picked = grad_all
    d_input = lax.psum_scatter(
        lax.dot_general(
            picked, weight, (((1,), (1,)), ((), ())), preferred_element_type=jnp.float32
        ),
        "col",
        scatter_dimension=0,
        tiled=True,
    ).astype(jnp.bfloat16)
    picked = grad_all
    summed = outer_block(lax.all_gather(activations, "col", axis=0, tiled=True), picked)
    return (d_input, summed.astype(jnp.bfloat16))


def solution(mesh):
    return jax.shard_map(
        on_device,
        mesh=mesh,
        in_specs=(P("col", "row"), P("row", "col"), P("row", "col")),
        out_specs=(P("col", "row"), P("row", "col")),
        check_vma=False,
    )
```

profile of v0, /device:TPU:24, one launch (start us, length us, event | category | flops | bytes accessed | tf_op | source)
XLA Modules:
  0.0 360.7 jit_solution(8364641244149399940)
XLA Ops:
  7.2 0.0 copy-start
  7.2 0.0 all-gather.3.cloned.1.call-start
  7.2 0.7 all-gather.3.cloned.1.call-update
  7.9 0.0 all-gather.5.cloned.1.call-start
  8.0 0.7 all-gather.5.cloned.1.call-update
  8.7 0.0 reduce-scatter.2.cloned.1.call-start
  8.7 69.4 %all-gather.3.cloned.1.call-done = bf16[1024,928]{1,0:T(8,128)(2,1)} async-done(((bf16[64,928]{1,0:T(8,128)(2,1)}), bf16[1024,928]{1,0:T(8,128)(2,1)}) %all-gather.3.cloned.1.call-update) | async-done | bytes 1900560 | tf_op jit(solution)/shard_map/all_gather | solution.py:14
  78.1 0.0 copy-done
  78.1 5.9 %fusion = f32[1024,928]{1,0:T(8,128)} fusion(bf16[1024,928]{1,0:T(8,128)(2,1)} %all-gather.3.cloned.1.call-done, bf16[928,928]{1,0:T(8,128)(2,1)S(1)} %copy-done), kind=kOutput, calls=%fused_computation.1 | convolution fusion | flops 1763704832 | bytes 7424000 | tf_op jit(solution)/shard_map/dot_general | solution.py:17
  84.0 0.0 reduce-scatter.2.cloned.1.call-update
  84.0 129.0 %all-gather.5.cloned.1.call-done = bf16[1024,928]{1,0:T(8,128)(2,1)} async-done(((bf16[32,928]{1,0:T(8,128)(2,1)}), bf16[1024,928]{1,0:T(8,128)(2,1)}) %all-gather.5.cloned.1.call-update) | async-done | bytes 1900560 | tf_op jit(solution)/shard_map/all_gather | solution.py:25
  213.1 5.7 %convolution_convert_fusion = bf16[928,928]{1,0:T(8,128)(2,1)} fusion(bf16[1024,928]{1,0:T(8,128)(2,1)} %all-gather.5.cloned.1.call-done, bf16[1024,928]{1,0:T(8,128)(2,1)} %all-gather.3.cloned.1.call-done), kind=kOutput, calls=%fused_computation | convolution fusion | flops 1764566016 | bytes 5523456 | tf_op jit(solution)/shard_map/dot_general | solution.py:8
  218.7 133.9 %reduce-scatter.2.cloned.1.call-done = f32[32,928]{1,0:T(8,128)} async-done(((f32[1024,928]{1,0:T(8,128)}), f32[32,928]{1,0:T(8,128)}) %reduce-scatter.2.cloned.1.call-update) | async-done | bytes 118800 | tf_op jit(solution)/shard_map/reduce_scatter | solution.py:16
  352.6 1.5 convert_element_type.6
Async XLA Ops:
  7.2 71.0 %copy-start = (bf16[928,928]{1,0:T(8,128)(2,1)S(1)}, bf16[928,928]{1,0:T(8,128)(2,1)}, u32[]{:S(2)}) copy-start(bf16[928,928]{1,0:T(8,128)(2,1)} %param.5) | copy-start | bytes 5167108
  7.2 70.9 %all-gather.3.cloned.1.call-start = ((), (), s32[]{:S(2)}) async-start(), calls=%async_computation.1 | async-start | bytes 2228224 | tf_op jit(solution)/shard_map/all_gather | solution.py:14
  7.9 205.1 %all-gather.5.cloned.1.call-start = ((), (), s32[]{:S(2)}) async-start(), calls=%async_computation.3 | async-start | bytes 2162688 | tf_op jit(solution)/shard_map/all_gather | solution.py:25
  8.7 343.9 %reduce-scatter.2.cloned.1.call-start = ((), (), s32[]{:S(2)}) async-start(), calls=%async_computation.2 | async-start | bytes 4325376 | tf_op jit(solution)/shard_map/reduce_scatter | solution.py:16
Sparse Core Ops, SparseCore 0:
  11.4 66.7 all-gather.2
  80.2 132.8 all-gather.4
  215.9 136.6 reduce-scatter.1
where the time goes:
time: 361 us
  waiting for transfers between devices  334 us (93%)
  between operations  13.8 us (4%)
  matrix products  11.6 us (3%)
    reduce_scatter x1, waiting for transfers between devices, on_device(): lax.psum_scatter(lax.dot_general(picked, weight, (((1,), (1,)), ((), ()))...  134 us
    all_gather x1, waiting for transfers between devices, on_device(): lax.all_gather(activations, 'col', axis=0, tiled=True)  129 us
    all_gather x1, waiting for transfers between devices, on_device(): grad_all = lax.all_gather(out_grad, 'row', axis=0, tiled=True)  69.4 us
  transfers between devices with their start and end apart: 3, of which 3 were waited for; matrix products, arithmetic and copies ran while one was open for 3% of the time, Pallas kernels for 0%

commit v1 on v0

v1 whole, which is shorter than its diff:
```python
import functools

import jax
import jax.numpy as jnp
from jax import lax
from jax.experimental import pallas as pl
from jax.experimental.pallas import tpu as pltpu
from jax.sharding import PartitionSpec as P

MESH = pl.DeviceIdType.MESH
F32 = jnp.float32
BF16 = jnp.bfloat16
Y, Z = 4, 16
HALF = Z // 2
T = 32
S = 16


def kernel(act_hbm, og_hbm, w_hbm, din_ref, dw_ref,
           act, og, w, part, xpart, ring, last,
           local_sem, r_send, r_recv, d_send, d_recv, a_send, a_recv, c_send, c_recv,
           x_send, x_recv, s_send, s_recv, l_send, l_recv):
    row, col = lax.axis_index("row"), lax.axis_index("col")
    xh, y, core = row // 8, (row // 2) % Y, row % 2
    xl, z = col // Z, col % Z

    def device(dx=0, dy=0, dcore=0, dl=0, dz=0):
        r = ((xh + dx) % 2) * 8 + ((y + dy) % Y) * 2 + (core + dcore) % 2
        c = ((xl + dl) % 2) * Z + (z + dz) % Z
        return (r, c)

    def owner_at(line, zz):
        return pl.multiple_of((zz // 4) * 256 + line * 128 + (zz % 4) * T, T)

    def source_at(hi, yy, cc):
        return pl.multiple_of(yy * 256 + hi * 128 + cc * 64, 64)

    def remote(src, dst, send, recv, **where):
        return pltpu.make_async_remote_copy(
            src_ref=src, dst_ref=dst, send_sem=send, recv_sem=recv,
            device_id=device(**where), device_id_type=MESH)

    own_og = og.at[pl.ds(source_at(xh, y, core), 64)]
    own_act = act.at[pl.ds(owner_at(xl, z), T)]
    get_og = pltpu.make_async_copy(og_hbm, own_og, local_sem.at[0])
    get_act = pltpu.make_async_copy(act_hbm, own_act, local_sem.at[1])
    get_w = pltpu.make_async_copy(w_hbm, w, local_sem.at[2])
    get_og.start()
    get_act.start()
    get_w.start()

    peers = [(dx, dy) for dy in (1, 3, 0, 2) for dx in (0, 1) if (dx, dy) != (0, 0)]
    barrier = pltpu.get_barrier_semaphore()
    near = [dict(dx=dx, dy=dy) for dx, dy in peers]
    near += [dict(dcore=1), dict(dl=1), dict(dz=1), dict(dz=Z - 1)]
    for where in near:
        pl.semaphore_signal(barrier, inc=1, device_id=device(**where), device_id_type=MESH)
    pl.semaphore_wait(barrier, len(near))

    waits = []

    def go(copy):
        copy.start()
        waits.append(copy)

    get_og.wait()
    for dx, dy in [(1, 0), (0, 1), (0, 3), (0, 2), (1, 1), (1, 3), (1, 2)]:
        go(remote(own_og, own_og, r_send.at[dx, dy], r_recv.at[dx, (Y - dy) % Y], dx=dx, dy=dy))
    go(remote(own_og, own_og, d_send.at[0, 0], d_recv.at[0, 0], dcore=1))

    get_act.wait()
    go(remote(own_act, own_act, a_send, a_recv, dl=1))

    def act_hop(line, way, step):
        zz = (z - (step - 1)) % Z if way == 0 else (z + (step - 1)) % Z
        block = act.at[pl.ds(owner_at((xl + line) % 2, zz), T)]
        return remote(block, block, c_send.at[line, way, step], c_recv.at[line, way, step],
                      dz=1 if way == 0 else Z - 1)

    hops = [HALF, HALF - 1]

    def act_step(line, step):
        for way in (0, 1):
            if step >= 2 and step - 1 <= hops[way]:
                act_hop(line, way, step - 1).wait_recv()
            if step <= hops[way]:
                go(act_hop(line, way, step))

    act_step(0, 1)
    remote(own_act, own_act, a_send, a_recv, dl=1).wait_recv()
    act_step(1, 1)

    def share(dx, dy):
        block = og.at[pl.ds(source_at((xh + dx) % 2, (y + dy) % Y, core), 64)]
        if (dx, dy) != (0, 0):
            remote(block, block, r_send.at[dx, dy], r_recv.at[dx, dy], dx=dx, dy=dy).wait_recv()
            go(remote(block, block, d_send.at[dx, dy], d_recv.at[dx, dy], dcore=1))

    def shared(dx, dy):
        block = og.at[pl.ds(source_at((xh + dx) % 2, (y + dy) % Y, (core + 1) % 2), 64)]
        remote(block, block, d_send.at[dx, dy], d_recv.at[dx, dy], dcore=1).wait_recv()

    def product(dy):
        rows = pl.ds(pl.multiple_of(((y + dy) % Y) * 256, 256), 256)
        part[rows, :] = lax.dot_general(
            og[rows, :], w[...], (((1,), (1,)), ((), ())), preferred_element_type=F32)

    def cross(dz):
        zz = (z + dz) % Z
        rows = part.at[pl.ds(owner_at((xl + 1) % 2, zz), S)]
        return remote(rows, xpart.at[zz], x_send.at[zz], x_recv.at[zz], dl=1)

    def cross_group(dy):
        for i in range(4):
            zz = ((y + dy) % Y) * 4 + i
            rows = part.at[pl.ds(owner_at((xl + 1) % 2, zz), S)]
            go(remote(rows, xpart.at[zz], x_send.at[zz], x_recv.at[zz], dl=1))

    share(1, 0)
    share(0, 1)
    share(0, 3)
    get_w.wait()
    shared(0, 0)
    shared(1, 0)
    product(0)
    cross_group(0)
    act_step(0, 2)
    act_step(1, 2)
    share(1, 1)
    share(1, 3)
    share(0, 2)
    share(1, 2)
    for dy in (1, 3, 2):
        for dx in (0, 1):
            shared(dx, dy)
        product(dy)
        cross_group(dy)
    act_step(0, 3)
    act_step(1, 3)

    def piece(p, zz):
        line = (xl + (1 if p == 1 else 0)) % 2
        return part.at[pl.ds(owner_at(line, zz) + (0 if p == 2 else S), S)]

    def sum_hop(way, k, p):
        d = HALF - k
        zz = (z + d) % Z if way == 0 else (z + Z - d) % Z
        src = piece(p, zz) if k == first[way] else ring.at[way, k - 1, p]
        return remote(src, ring.at[way, k, p], s_send.at[way, k, p], s_recv.at[way, k, p],
                      dz=1 if way == 0 else Z - 1)

    first = [0, 1]

    def sum_step(k):
        for p in range(3):
            for way in (0, 1):
                if k < first[way]:
                    continue
                d = HALF - k
                zz = (z + d) % Z if way == 0 else (z + Z - d) % Z
                mine = piece(p, zz)
                if p == 2:
                    cross(d if way == 0 else Z - d).wait_recv()
                    mine[...] += xpart[zz]
                if k > first[way]:
                    sum_hop(way, k - 1, p).wait_recv()
                    ring[way, k - 1, p] = ring[way, k - 1, p] + mine[...]
                go(sum_hop(way, k, p))

    def weight_grad(start, width):
        cols = pl.ds(start, width)
        dw_ref[:, cols] = lax.dot_general(
            act[...], og[:, cols], (((0,), (0,)), ((), ())),
            preferred_element_type=F32).astype(BF16)

    for k in range(HALF):
        sum_step(k)
        if k + 4 <= HALF + 1:
            act_step(0, k + 4)
            act_step(1, k + 4)
        if k == 6:
            weight_grad(0, 256)
            weight_grad(256, 256)
        if k == 7:
            weight_grad(512, 256)
            weight_grad(768, 160)

    def total(p):
        mine = piece(p, z)
        acc = mine[...]
        if p == 2:
            cross(0).wait_recv()
            acc += xpart[z]
        for way in (0, 1):
            sum_hop(way, HALF - 1, p).wait_recv()
            acc += ring[way, HALF - 1, p]
        return acc

    other = total(1)
    mine = piece(1, z)
    mine[...] = other
    swap = remote(mine, last, l_send, l_recv, dl=1)
    go(swap)
    acc = total(0)
    din_ref[:S, :] = total(2).astype(BF16)
    swap.wait_recv()
    din_ref[S:, :] = (acc + last[...]).astype(BF16)
    for copy in waits:
        copy.wait_send()


def on_device(activations, out_grad, weight):
    model, hidden = weight.shape
    dma = pltpu.SemaphoreType.DMA
    return pl.pallas_call(
        kernel,
        out_shape=(jax.ShapeDtypeStruct(activations.shape, BF16), jax.ShapeDtypeStruct(weight.shape, BF16)),
        in_specs=[pl.BlockSpec(memory_space=pl.ANY)] * 3,
        out_specs=(pl.BlockSpec(memory_space=pltpu.VMEM), pl.BlockSpec(memory_space=pltpu.VMEM)),
        scratch_shapes=[
            pltpu.VMEM((2 * Z * T, model), BF16),
            pltpu.VMEM((2 * Z * T, hidden), BF16),
            pltpu.VMEM((model, hidden), BF16),
            pltpu.VMEM((2 * Z * T, model), F32),
            pltpu.VMEM((Z, S, model), F32),
            pltpu.VMEM((2, HALF, 3, S, model), F32),
            pltpu.VMEM((S, model), F32),
            dma((3,)),
            dma((2, Y)), dma((2, Y)),
            dma((2, Y)), dma((2, Y)),
            dma(()), dma(()),
            dma((2, 2, HALF + 1)), dma((2, 2, HALF + 1)),
            dma((Z,)), dma((Z,)),
            dma((2, HALF, 3)), dma((2, HALF, 3)),
            dma(()), dma(()),
        ],
        compiler_params=pltpu.CompilerParams(
            collective_id=0, has_side_effects=True, vmem_limit_bytes=48 << 20),
        name="backward",
    )(activations, out_grad, weight)


def solution(mesh):
    return jax.shard_map(
        on_device,
        mesh=mesh,
        in_specs=(P("col", "row"), P("row", "col"), P("row", "col")),
        out_specs=(P("col", "row"), P("row", "col")),
        check_vma=False,
    )
```

time: 361 us -> 110 us (0.30)
  waiting for transfers between devices: 334 us -> 0 us
  Pallas kernels: 0 us -> 104 us
  between operations: 13.8 us -> 0.65 us
  matrix products: 11.6 us -> 0 us
  local copies, waits for them, and re-layouts: 0.01 us -> 5.14 us
    all_gather x2 -> x0, waiting for transfers between devices: 198 us -> none  [the longest x1 129 us: on_device(): lax.all_gather(activations, 'col', axis=0, tiled=True)]
    reduce_scatter x1 -> x0, waiting for transfers between devices: 134 us -> none  [on_device(): lax.psum_scatter(lax.dot_general(picked, weight, (((1,), (1,)), ((), ()))...]
    pallas_call x0 -> x1, Pallas kernels: none -> 104 us  [on_device(): pl.pallas_call(kernel, out_shape=(jax.ShapeDtypeStruct(activations.shape,...]
    dot_general x2 -> x0, matrix products: 11.6 us -> none  [the longest x1 5.9 us: on_device(): lax.dot_general(picked, weight, (((1,), (1,)), ((), ())), preferred_eleme...]
    unnamed x2 -> x8, local copies, waits for them, and re-layouts: 0.01 us -> 5.14 us
  transfers between devices with their start and end apart: 3 -> 0, of which waited for: 3 -> 0; matrix products, arithmetic and copies ran while one was open for 3% -> 0% of each run, Pallas kernels for 0% -> 0%
where the time goes in v1:
time: 110 us
  Pallas kernels  104 us (95%)
  local copies, waits for them, and re-layouts  5.14 us (5%)
    pallas_call x1, Pallas kernels, on_device(): pl.pallas_call(kernel, out_shape=(jax.ShapeDtypeStruct(activations.shape,...  104 us
    unnamed x8, local copies, waits for them, and re-layouts  5.14 us

profile of v1, /device:TPU:24, one launch (start us, length us, event | category | flops | bytes accessed | tf_op | source)
XLA Modules:
  0.0 109.7 jit_solution(9012531251568053775)
XLA Ops:
  0.6 0.0 copy-start
  0.6 1.5 %copy-done = bf16[928,928]{1,0:T(8,128)(2,1)S(1)} copy-done((bf16[928,928]{1,0:T(8,128)(2,1)S(1)}, bf16[928,928]{1,0:T(8,128)(2,1)}, u32[]{:S(2)}) %copy-start) | copy-done | bytes 1722392
  2.2 0.0 copy-start.1
  2.2 0.9 copy-done.1
  3.1 0.0 copy-start.2
  3.1 0.8 copy-done.2
  3.9 103.9 %backward.1 = (bf16[32,928]{1,0:T(8,128)(2,1)S(1)}, bf16[928,928]{1,0:T(8,128)(2,1)S(1)}) custom-call(bf16[32,928]{1,0:T(8,128)(2,1)S(1)} %copy-done.2, bf16[64,928]{1,0:T(8,128)(2,1)S(1)} %copy-done.1, bf16[928,928]{1,0:T(8,128)(2,1)S(1)} %copy-done), custom_call_target="tpu_custom_call" | custom-call | tf_op jit(solution)/shard_map/backward/pallas_call | solution.py:215
  107.8 0.6 copy.7
  108.5 1.2 %copy.8 = bf16[928,928]{1,0:T(8,128)(2,1)} copy(bf16[928,928]{1,0:T(8,128)(2,1)S(1)} %get-tuple-element.5) | data formatting | bytes 3444736
Async XLA Ops:
  0.6 1.5 %copy-start = (bf16[928,928]{1,0:T(8,128)(2,1)S(1)}, bf16[928,928]{1,0:T(8,128)(2,1)}, u32[]{:S(2)}) copy-start(bf16[928,928]{1,0:T(8,128)(2,1)} %w_hbm.1) | copy-start | bytes 5167108
  2.2 0.9 copy-start.1
  3.1 0.8 copy-start.2

commit v2 on v0

v2 whole, which is shorter than its diff:
```python
import jax
import jax.numpy as jnp
from jax import lax
from jax.experimental import pallas as pl
from jax.experimental.pallas import tpu as pltpu
from jax.sharding import PartitionSpec as P

MESH = pl.DeviceIdType.MESH
F32 = jnp.float32
BF16 = jnp.bfloat16
FLAGS = set()
Y, Z = 4, 16
HALF = Z // 2
WIDE = 7
MAIN = WIDE * 128
OG = 4 * WIDE + 1
ACT = 2 * WIDE + 1
SUM = 4 * WIDE + 1
OG_CUT = (0, 2 * WIDE, OG)
ACT_X = 8
SUM_X = 18
LAST = SUM - SUM_X
PIECES = (
    (0, SUM_X, LAST, 1),
    (LAST, SUM_X, LAST, 0),
    (2 * LAST, 0, SUM_X // 2, 0),
    (2 * LAST + SUM_X // 2, SUM_X // 2, SUM_X - SUM_X // 2, 0),
)
SLOT = 2 * LAST + SUM_X
FIRST = ((0, 1), (0, 1), (1, 0), (1, 0))


def kernel(act_hbm, og_hbm, w_hbm, din_ref, dw_hbm,
           act, og, w, wtail, act_pk, og_pk, part, xpart, ring, last, dw,
           local_sem, out_sem, r_send, r_recv, d_send, d_recv, a_send, a_recv, b_send, b_recv,
           c_send, c_recv, x_send, x_recv, s_send, s_recv, l_send, l_recv):
    row, col = lax.axis_index("row"), lax.axis_index("col")
    xh, y, core = row // 8, (row // 2) % Y, row % 2
    xl, z = col // Z, col % Z

    def device(dx=0, dy=0, dcore=0, dl=0, dz=0):
        r = ((xh + dx) % 2) * 8 + ((y + dy) % Y) * 2 + (core + dcore) % 2
        c = ((xl + dl) % 2) * Z + (z + dz) % Z
        return (r, c)

    def owner_at(line, zz):
        return (zz // 4) * 8 + line * 4 + zz % 4

    def source_at(hi, yy, cc):
        return yy * 4 + hi * 2 + cc

    def remote(src, dst, send, recv, **where):
        return pltpu.make_async_remote_copy(
            src_ref=src, dst_ref=dst, send_sem=send, recv_sem=recv,
            device_id=device(**where), device_id_type=MESH)

    waits = []

    def go(copy):
        copy.start()
        waits.append(copy)

    mine_og, mine_act = source_at(xh, y, core), owner_at(xl, z)
    get_og = pltpu.make_async_copy(
        og_hbm, og.at[pl.ds(pl.multiple_of(mine_og * 64, 64), 64)], local_sem.at[0])
    get_act = pltpu.make_async_copy(
        act_hbm, act.at[pl.ds(pl.multiple_of(mine_act * 32, 32), 32)], local_sem.at[1])
    get_w = pltpu.make_async_copy(w_hbm, w, local_sem.at[2])
    get_og.start()
    get_act.start()
    get_w.start()

    barrier = pltpu.get_barrier_semaphore()
    near = [dict(dx=1), dict(dy=1), dict(dy=3), dict(dy=2),
            dict(dcore=1), dict(dl=1), dict(dz=1), dict(dz=Z - 1)]
    for where in near:
        pl.semaphore_signal(barrier, inc=1, device_id=device(**where), device_id_type=MESH)

    def pack(rows_ref, base, groups, pk, place):
        tails = []
        for i in range(groups):
            rows = pl.ds(pl.multiple_of(base + 16 * i, 16), 16)
            for j in range(WIDE):
                pk[place, i * WIDE + j] = rows_ref[rows, j * 128:(j + 1) * 128]
            tails.append(rows_ref[rows, MAIN:])
        pk[place, groups * WIDE, :, :32 * groups] = jnp.concatenate(tails, axis=1)

    def unpack(pk, place, groups, rows_ref, base):
        tails = pk[place, groups * WIDE]
        for i in range(groups):
            rows = pl.ds(pl.multiple_of(base + 16 * i, 16), 16)
            for j in range(WIDE):
                rows_ref[rows, j * 128:(j + 1) * 128] = pk[place, i * WIDE + j]
            rows_ref[rows, MAIN:] = tails[:, 32 * i:32 * (i + 1)]

    get_og.wait()
    pack(og, mine_og * 64, 4, og_pk, mine_og)
    get_act.wait()
    pack(act, mine_act * 32, 2, act_pk, mine_act)
    pl.semaphore_wait(barrier, len(near))

    def og_piece(dx, dy, dcore, p):
        place = source_at((xh + dx) % 2, (y + dy) % Y, (core + dcore) % 2)
        return og_pk.at[place, pl.ds(OG_CUT[p], OG_CUT[p + 1] - OG_CUT[p])]

    def to_x(p):
        ref = og_piece(0, 0, 0, p)
        return remote(ref, ref, r_send.at[1, 0, p], r_recv.at[1, 0, p], dx=1)

    def to_y(dx, dy, p):
        ref = og_piece(dx, 0, 0, p)
        return remote(ref, ref, r_send.at[dx, dy, p], r_recv.at[dx, (Y - dy) % Y, p], dy=dy)

    def to_core(dx, dy, p):
        ref = og_piece(dx, dy, 0, p)
        return remote(ref, ref, d_send.at[dx, dy, p], d_recv.at[dx, dy, p], dcore=1)

    def arrived(dx, dy, p):
        ref = og_piece(dx, dy, 0, p)
        remote(ref, ref, r_send.at[dx, dy, p], r_recv.at[dx, dy, p], dx=1).wait_recv()

    def shared(dx, dy, p):
        ref = og_piece(dx, dy, 1, p)
        remote(ref, ref, d_send.at[dx, dy, p], d_recv.at[dx, dy, p], dcore=1).wait_recv()

    for p in (0, 1):
        go(to_x(p))
    for p in (0, 1):
        for dy in (1, 3):
            go(to_y(0, dy, p))
    for p in (0, 1):
        go(to_y(0, 2, p))

    def act_x(first_tiles, zz):
        cut = pl.ds(0, ACT_X) if first_tiles else pl.ds(ACT_X, ACT - ACT_X)
        ref = act_pk.at[owner_at(xl, zz), cut]
        if first_tiles:
            return remote(ref, ref, a_send, a_recv, dl=1)
        return remote(ref, ref, b_send.at[zz], b_recv.at[zz], dl=1)

    def act_hop(line, way, step):
        zz = (z - (step - 1)) % Z if way == 0 else (z + (step - 1)) % Z
        ref = act_pk.at[owner_at((xl + line) % 2, zz), pl.ds(0, ACT if line == 0 else ACT_X)]
        return remote(ref, ref, c_send.at[line, way, step], c_recv.at[line, way, step],
                      dz=1 if way == 0 else Z - 1)

    hops = (HALF, HALF - 1)

    def act_step(line, step):
        if "noC" in FLAGS:
            return
        for way in (0, 1):
            if step >= 2 and step - 1 <= hops[way]:
                act_hop(line, way, step - 1).wait_recv()
            if step <= hops[way]:
                go(act_hop(line, way, step))
            if line == 0 and step >= 2 and step - 1 <= hops[way]:
                go(act_x(False, (z - (step - 1)) % Z if way == 0 else (z + (step - 1)) % Z))

    go(act_x(True, z))
    act_step(0, 1)
    go(act_x(False, z))
    for p in (0, 1):
        go(to_core(0, 0, p))

    get_w.wait()
    for i in range(4):
        wtail[32 * i:32 * (i + 1), :] = w[MAIN:, :]

    for p in (0, 1):
        arrived(1, 0, p)
        for dy in (1, 3, 2):
            go(to_y(1, dy, p))
        go(to_core(1, 0, p))
    act_x(True, z).wait_recv()
    act_step(1, 1)
    for p in (0, 1):
        for dy in (1, 3):
            arrived(0, dy, p)
            go(to_core(0, dy, p))

    lane = lax.broadcasted_iota(jnp.int32, (8, 128), 1) // 32

    def product(dy):
        group = (y + dy) % Y
        if "noP" in FLAGS:
            return
        for i in range(4):
            unpack(og_pk, group * 4 + i, 4, og, (group * 4 + i) * 64)
        left = og[pl.ds(pl.multiple_of(group * 256, 256), 256), :]
        for j in range(0, WIDE + 1, 2):
            if j + 1 < WIDE:
                right = w[j * 128:(j + 2) * 128, :]
            else:
                right = jnp.concatenate([w[j * 128:(j + 1) * 128, :], wtail[...]], axis=0)
            out = lax.dot_general(left, right, (((1,), (1,)), ((), ())), preferred_element_type=F32)
            for q in range(8):
                rows = out[q * 32:(q + 1) * 32]
                part[group * 8 + q, j * 4:(j + 1) * 4] = rows[:, :128].reshape(4, 8, 128)
                if j + 1 < WIDE:
                    part[group * 8 + q, (j + 1) * 4:(j + 2) * 4] = rows[:, 128:].reshape(4, 8, 128)
                else:
                    tail = rows[:, 128:].reshape(4, 8, 128)
                    packed = tail[0]
                    for i in range(1, 4):
                        packed = jnp.where(lane == i, tail[i], packed)
                    part[group * 8 + q, 4 * WIDE] = packed

    def cross(zz):
        return remote(part.at[owner_at((xl + 1) % 2, zz), pl.ds(0, SUM_X)], xpart.at[zz],
                      x_send.at[zz], x_recv.at[zz], dl=1)

    def group_of(dy):
        for dx in (0, 1):
            for p in (0, 1):
                shared(dx, dy, p)
        product(dy)

    group_of(0)
    act_step(0, 2)
    act_step(1, 2)
    for p in (0, 1):
        arrived(0, 2, p)
        go(to_core(0, 2, p))
    for dy in (1, 3):
        for p in (0, 1):
            arrived(1, dy, p)
            go(to_core(1, dy, p))
    group_of(1)
    group_of(3)
    for p in (0, 1):
        arrived(1, 2, p)
        go(to_core(1, 2, p))
    act_step(0, 3)
    act_step(1, 3)
    group_of(2)
    for d in range(HALF, 0, -1):
        if "noX" in FLAGS: continue
        go(cross((z + d) % Z))
        if d < HALF:
            go(cross((z + Z - d) % Z))
    if "noX" not in FLAGS: go(cross(z))

    def mine_of(p, zz):
        _, start, size, line = PIECES[p]
        return part.at[owner_at((xl + line) % 2, zz), pl.ds(start, size)]

    def owner_on(way, k):
        d = HALF - k
        return (z + d) % Z if way == 0 else (z + Z - d) % Z

    def sum_hop(way, k, p):
        place, _, size, _ = PIECES[p]
        cut = pl.ds(place, size)
        src = mine_of(p, owner_on(way, k)) if k == FIRST[p][way] else ring.at[way, k - 1, cut]
        return remote(src, ring.at[way, k, cut], s_send.at[way, k, p], s_recv.at[way, k, p],
                      dz=1 if way == 0 else Z - 1)

    def sum_step(k):
        for p in range(4):
            place, start, size, line = PIECES[p]
            for way in (0, 1):
                if k < FIRST[p][way]:
                    continue
                zz = owner_on(way, k)
                mine = mine_of(p, zz)
                if p == 2:
                    cross(zz).wait_recv()
                if k > FIRST[p][way]:
                    sum_hop(way, k - 1, p).wait_recv()
                    cut = pl.ds(place, size)
                    acc = ring[way, k - 1, cut] + mine[...]
                    if p >= 2:
                        acc += xpart[zz, start:start + size]
                    ring[way, k - 1, cut] = acc
                elif p >= 2:
                    mine[...] += xpart[zz, start:start + size]
                go(sum_hop(way, k, p))

    def weight_grad(start, width):
        cols = pl.ds(start, width)
        dw[:, cols] = lax.dot_general(
            act[...], og[:, cols], (((0,), (0,)), ((), ())),
            preferred_element_type=F32).astype(BF16)
        pltpu.make_async_copy(dw.at[:, cols], dw_hbm.at[:, cols], out_sem.at[start // 256]).start()

    for k in range(HALF):
        if "noS" not in FLAGS:
            sum_step(k)
        if k + 4 <= HALF + 1:
            act_step(0, k + 4)
            act_step(1, k + 4)
        if "noDW" in FLAGS:
            continue
        if k == 6:
            for zz in range(Z):
                other = act_pk.at[owner_at((xl + 1) % 2, zz), pl.ds(ACT_X, ACT - ACT_X)]
                remote(other, other, b_send.at[zz], b_recv.at[zz], dl=1).wait_recv()

            @pl.loop(0, 2 * Z)
            def _(place):
                unpack(act_pk, place, 2, act, place * 32)

            weight_grad(0, 256)
            weight_grad(256, 256)
        if k == 7:
            weight_grad(512, 256)
            weight_grad(768, 160)

    def total(p):
        place, start, size, line = PIECES[p]
        acc = mine_of(p, z)[...]
        if p == 2:
            cross(z).wait_recv()
        if p >= 2:
            acc += xpart[z, start:start + size]
        for way in (0, 1):
            if "noS" in FLAGS:
                continue
            sum_hop(way, HALF - 1, p).wait_recv()
            acc += ring[way, HALF - 1, pl.ds(place, size)]
        return acc

    other = mine_of(0, z)
    other[...] = total(0)
    swap = remote(other, last, l_send, l_recv, dl=1)
    go(swap)

    def tiles_out(acc, start):
        for t in range(acc.shape[0]):
            j, i = (start + t) // 4, (start + t) % 4
            if j < WIDE:
                din_ref[8 * i:8 * (i + 1), j * 128:(j + 1) * 128] = acc[t].astype(BF16)
            else:
                for i in range(4):
                    din_ref[8 * i:8 * (i + 1), MAIN:] = acc[t][:, 32 * i:32 * (i + 1)].astype(BF16)

    acc = total(1)
    tiles_out(total(2), 0)
    tiles_out(total(3), SUM_X // 2)
    swap.wait_recv()
    tiles_out(acc + last[...], SUM_X)
    if "noDW" not in FLAGS:
        for i, width in enumerate((256, 256, 256, 160)):
            cols = pl.ds(256 * i, width)
            pltpu.make_async_copy(dw.at[:, cols], dw_hbm.at[:, cols], out_sem.at[i]).wait()
    else:
        for zz in range(Z):
            other = act_pk.at[owner_at((xl + 1) % 2, zz), pl.ds(ACT_X, ACT - ACT_X)]
            if "noC" not in FLAGS: remote(other, other, b_send.at[zz], b_recv.at[zz], dl=1).wait_recv()
    for copy in waits:
        copy.wait_send()


def on_device(activations, out_grad, weight):
    model, hidden = weight.shape
    dma = pltpu.SemaphoreType.DMA
    return pl.pallas_call(
        kernel,
        out_shape=(jax.ShapeDtypeStruct(activations.shape, BF16), jax.ShapeDtypeStruct(weight.shape, BF16)),
        in_specs=[pl.BlockSpec(memory_space=pl.ANY)] * 3,
        out_specs=(pl.BlockSpec(memory_space=pltpu.VMEM), pl.BlockSpec(memory_space=pl.ANY)),
        scratch_shapes=[
            pltpu.VMEM((2 * Z * 32, model), BF16),
            pltpu.VMEM((2 * Z * 32, hidden), BF16),
            pltpu.VMEM((model, hidden), BF16),
            pltpu.VMEM((128, hidden), BF16),
            pltpu.VMEM((2 * Z, ACT, 16, 128), BF16),
            pltpu.VMEM((4 * Y, OG, 16, 128), BF16),
            pltpu.VMEM((2 * Z, SUM, 8, 128), F32),
            pltpu.VMEM((Z, SUM_X, 8, 128), F32),
            pltpu.VMEM((2, HALF, SLOT, 8, 128), F32),
            pltpu.VMEM((LAST, 8, 128), F32),
            pltpu.VMEM((model, hidden), BF16),
            dma((3,)), dma((4,)),
            dma((2, Y, 2)), dma((2, Y, 2)),
            dma((2, Y, 2)), dma((2, Y, 2)),
            dma(()), dma(()),
            dma((Z,)), dma((Z,)),
            dma((2, 2, HALF + 1)), dma((2, 2, HALF + 1)),
            dma((Z,)), dma((Z,)),
            dma((2, HALF, 4)), dma((2, HALF, 4)),
            dma(()), dma(()),
        ],
        compiler_params=pltpu.CompilerParams(
            collective_id=0, has_side_effects=True, vmem_limit_bytes=60 << 20),
        name="backward",
    )(activations, out_grad, weight)


def solution(mesh):
    return jax.shard_map(
        on_device,
        mesh=mesh,
        in_specs=(P("col", "row"), P("row", "col"), P("row", "col")),
        out_specs=(P("col", "row"), P("row", "col")),
        check_vma=False,
    )
```

time: 361 us -> 81.6 us (0.23)
  waiting for transfers between devices: 334 us -> 0 us
  Pallas kernels: 0 us -> 75.1 us
  between operations: 13.8 us -> 0.64 us
  matrix products: 11.6 us -> 0 us
  local copies, waits for them, and re-layouts: 0.01 us -> 4.39 us
    all_gather x2 -> x0, waiting for transfers between devices: 198 us -> none  [the longest x1 129 us: on_device(): lax.all_gather(activations, 'col', axis=0, tiled=True)]
    reduce_scatter x1 -> x0, waiting for transfers between devices: 134 us -> none  [on_device(): lax.psum_scatter(lax.dot_general(picked, weight, (((1,), (1,)), ((), ()))...]
    pallas_call x0 -> x1, Pallas kernels: none -> 75.1 us  [on_device(): pl.pallas_call(kernel, out_shape=(jax.ShapeDtypeStruct(activations.shape,...]
    dot_general x2 -> x0, matrix products: 11.6 us -> none  [the longest x1 5.9 us: on_device(): lax.dot_general(picked, weight, (((1,), (1,)), ((), ())), preferred_eleme...]
    unnamed x2, local copies, waits for them, and re-layouts: 0.01 us -> 4.39 us
  transfers between devices with their start and end apart: 3 -> 0, of which waited for: 3 -> 0; matrix products, arithmetic and copies ran while one was open for 3% -> 0% of each run, Pallas kernels for 0% -> 0%
where the time goes in v2:
time: 81.6 us; the launch traced here: 80.1 us
  Pallas kernels  75.1 us (92%)
  local copies, waits for them, and re-layouts  4.39 us (5%)
    pallas_call x1, Pallas kernels, on_device(): pl.pallas_call(kernel, out_shape=(jax.ShapeDtypeStruct(activations.shape,...  75.1 us
    unnamed x2, local copies, waits for them, and re-layouts  4.39 us

profile of v2, /device:TPU:24, one launch (start us, length us, event | category | flops | bytes accessed | tf_op | source)
XLA Modules:
  0.0 80.1 jit_solution(17412692368287142128)
XLA Ops:
  0.6 75.1 %backward.1 = (bf16[32,928]{1,0:T(8,128)(2,1)}, bf16[928,928]{1,0:T(8,128)(2,1)}) custom-call(bf16[32,928]{1,0:T(8,128)(2,1)} %act_hbm.1, bf16[64,928]{1,0:T(8,128)(2,1)} %og_hbm.1, bf16[928,928]{1,0:T(8,128)(2,1)} %w_hbm.1), custom_call_target="tpu_custom_call" | custom-call | tf_op jit(solution)/shard_map/backward/pallas_call | solution.py:358
  75.7 1.5 %copy.7 = bf16[32,928]{1,0:T(8,128)(2,1)} copy(bf16[32,928]{1,0:T(8,128)(2,1)} %get-tuple-element.4) | data formatting | bytes 118784
  77.2 2.9 %copy.8 = bf16[928,928]{1,0:T(8,128)(2,1)} copy(bf16[928,928]{1,0:T(8,128)(2,1)} %get-tuple-element.5) | data formatting | bytes 3444736

commit v3 on v2

v3 whole, which is shorter than its diff:
```python
import jax
import jax.numpy as jnp
from jax import lax
from jax.experimental import pallas as pl
from jax.experimental.pallas import tpu as pltpu
from jax.sharding import PartitionSpec as P

MESH = pl.DeviceIdType.MESH
F32 = jnp.float32
BF16 = jnp.bfloat16
FLAGS = set()
Y, Z = 4, 16
HALF = Z // 2
WIDE = 7
MAIN = WIDE * 128
OG = 4 * WIDE + 1
ACT = 2 * WIDE + 1
ACT_CUT = (0, 8, ACT)
SUM = 4 * WIDE + 1
OG_CUT = (0, 2 * WIDE, OG)
SUM = 2 * WIDE + 1
SPAN = 200.0
FIRST = ((0, 1), (1, 0))


def encode(total, tail):
    top = jnp.maximum(jnp.max(jnp.abs(total.reshape(-1, 8, 128)), axis=0), jnp.abs(tail))
    scale = jnp.maximum(top * 1.01, 1e-30).astype(BF16)
    inverse = SPAN / scale.astype(F32)

    def code(values):
        power = values * inverse
        number = jnp.exp2(jnp.abs(power) - SPAN / 2)
        return jnp.where(power < 0, -number, number)

    main = code(total.reshape(-1, 8, 128)).reshape(total.shape).astype(BF16)
    return main, jnp.concatenate([code(tail), scale.astype(F32)], axis=0).astype(BF16)


def decode(main, rest):
    rest = rest.astype(F32)
    step = rest[8:] * (1 / SPAN)

    def value(number):
        size = jnp.log(jnp.abs(number)) * 1.4426950408889634 + SPAN / 2
        return jnp.where(number < 0, -size, size) * step

    main = main.astype(F32)
    return value(main.reshape(-1, 8, 128)).reshape(main.shape), value(rest[:8])


def kernel(act_hbm, og_hbm, w_hbm, din_ref, dw_hbm,
           act, og, w, wtail, act_pk, og_pk, part, ring, out, last, dw,
           local_sem, out_sem, r_send, r_recv, d_send, d_recv, b_send, b_recv,
           c_send, c_recv, s_send, s_recv, l_send, l_recv):
    row, col = lax.axis_index("row"), lax.axis_index("col")
    xh, y, core = row // 8, (row // 2) % Y, row % 2
    xl, z = col // Z, col % Z

    def device(dx=0, dy=0, dcore=0, dl=0, dz=0):
        r = ((xh + dx) % 2) * 8 + ((y + dy) % Y) * 2 + (core + dcore) % 2
        c = ((xl + dl) % 2) * Z + (z + dz) % Z
        return (r, c)

    def owner_at(line, zz):
        return (zz // 4) * 8 + line * 4 + zz % 4

    def source_at(hi, yy, cc):
        return yy * 4 + hi * 2 + cc

    def remote(src, dst, send, recv, **where):
        return pltpu.make_async_remote_copy(
            src_ref=src, dst_ref=dst, send_sem=send, recv_sem=recv,
            device_id=device(**where), device_id_type=MESH)

    waits = []

    def go(copy):
        copy.start()
        waits.append(copy)

    mine_og, mine_act = source_at(xh, y, core), owner_at(xl, z)
    get_og = pltpu.make_async_copy(
        og_hbm, og.at[pl.ds(pl.multiple_of(mine_og * 64, 64), 64)], local_sem.at[0])
    get_act = pltpu.make_async_copy(
        act_hbm, act.at[pl.ds(pl.multiple_of(mine_act * 32, 32), 32)], local_sem.at[1])
    get_w = pltpu.make_async_copy(w_hbm, w, local_sem.at[2])
    get_og.start()
    get_act.start()
    get_w.start()

    barrier = pltpu.get_barrier_semaphore()
    near = [dict(dx=1), dict(dy=1), dict(dy=3), dict(dy=2),
            dict(dcore=1), dict(dl=1), dict(dz=1), dict(dz=Z - 1),
            dict(dl=1, dz=1), dict(dl=1, dz=Z - 1)]
    for where in near:
        pl.semaphore_signal(barrier, inc=1, device_id=device(**where), device_id_type=MESH)

    def pack(rows_ref, base, groups, pk, place):
        tails = []
        for i in range(groups):
            rows = pl.ds(pl.multiple_of(base + 16 * i, 16), 16)
            for j in range(WIDE):
                pk[place, i * WIDE + j] = rows_ref[rows, j * 128:(j + 1) * 128]
            tails.append(rows_ref[rows, MAIN:])
        pk[place, groups * WIDE, :, :32 * groups] = jnp.concatenate(tails, axis=1)

    def unpack(pk, place, groups, rows_ref, base):
        tails = pk[place, groups * WIDE]
        for i in range(groups):
            rows = pl.ds(pl.multiple_of(base + 16 * i, 16), 16)
            for j in range(WIDE):
                rows_ref[rows, j * 128:(j + 1) * 128] = pk[place, i * WIDE + j]
            rows_ref[rows, MAIN:] = tails[:, 32 * i:32 * (i + 1)]

    get_og.wait()
    pack(og, mine_og * 64, 4, og_pk, mine_og)
    get_act.wait()
    pack(act, mine_act * 32, 2, act_pk, mine_act)
    pl.semaphore_wait(barrier, len(near))

    def og_piece(dx, dy, dcore, p):
        place = source_at((xh + dx) % 2, (y + dy) % Y, (core + dcore) % 2)
        return og_pk.at[place, pl.ds(OG_CUT[p], OG_CUT[p + 1] - OG_CUT[p])]

    def to_x(p):
        ref = og_piece(0, 0, 0, p)
        return remote(ref, ref, r_send.at[1, 0, p], r_recv.at[1, 0, p], dx=1)

    def to_y(dx, dy, p):
        ref = og_piece(dx, 0, 0, p)
        return remote(ref, ref, r_send.at[dx, dy, p], r_recv.at[dx, (Y - dy) % Y, p], dy=dy)

    def over_x(p):
        ref = og_piece(0, 2, 0, p)
        return remote(ref, ref, r_send.at[1, 2, p], r_recv.at[1, 2, p], dx=1)

    def to_core(dx, dy, p):
        ref = og_piece(dx, dy, 0, p)
        return remote(ref, ref, d_send.at[dx, dy, p], d_recv.at[dx, dy, p], dcore=1)

    def arrived(dx, dy, p):
        ref = og_piece(dx, dy, 0, p)
        remote(ref, ref, r_send.at[dx, dy, p], r_recv.at[dx, dy, p], dx=1).wait_recv()

    def shared(dx, dy, p):
        ref = og_piece(dx, dy, 1, p)
        remote(ref, ref, d_send.at[dx, dy, p], d_recv.at[dx, dy, p], dcore=1).wait_recv()

    for p in (0, 1):
        go(to_x(p))
    for p in (0, 1):
        for dy in (1, 3):
            go(to_y(0, dy, p))
    for p in (0, 1):
        go(to_y(0, 2, p))

    def act_piece(line, zz, p):
        return act_pk.at[owner_at((xl + line) % 2, zz), pl.ds(ACT_CUT[p], ACT_CUT[p + 1] - ACT_CUT[p])]

    def act_x(line, zz, p):
        ref = act_piece(line, zz, p)
        return remote(ref, ref, b_send.at[zz, p], b_recv.at[zz, p], dl=1)

    def back(way, step):
        return (z - step) % Z if way == 0 else (z + step) % Z

    def act_hop(way, step, p):
        ref = act_piece(0, back(way, step - 1), p)
        return remote(ref, ref, c_send.at[way, step, p], c_recv.at[way, step, p], dz=1 if way == 0 else Z - 1)

    hops = (HALF, HALF - 1)

    def act_step(step):
        if "noC" in FLAGS:
            return
        for p in (0, 1):
            for way in (0, 1):
                if 2 <= step <= hops[way] + 1:
                    act_hop(way, step - 1, p).wait_recv()
                if step <= hops[way]:
                    go(act_hop(way, step, p))
        for p in (0, 1):
            for way in (0, 1):
                if 2 <= step <= hops[way] + 1:
                    go(act_x(0, back(way, step - 1), p))

    act_step(1)
    if "noC" not in FLAGS:
        for p in (0, 1):
            go(act_x(0, z, p))
    for p in (0, 1):
        go(to_core(0, 0, p))

    get_w.wait()
    for i in range(4):
        wtail[32 * i:32 * (i + 1), :] = w[MAIN:, :]

    for p in (0, 1):
        arrived(1, 0, p)
        for dy in (1, 3):
            go(to_y(1, dy, p))
        if p == 0:
            go(to_y(1, 2, p))
        go(to_core(1, 0, p))
    for p in (0, 1):
        for dy in (1, 3):
            arrived(0, dy, p)
            go(to_core(0, dy, p))
    for p in (1, 0):
        arrived(0, 2, p)
        if p == 1:
            go(over_x(p))
        go(to_core(0, 2, p))
    act_step(2)

    lane = lax.broadcasted_iota(jnp.int32, (8, 128), 1) // 32

    def product(dy):
        group = (y + dy) % Y
        if "noP" in FLAGS:
            return
        for i in range(4):
            unpack(og_pk, group * 4 + i, 4, og, (group * 4 + i) * 64)
        left = og[pl.ds(pl.multiple_of(group * 256, 256), 256), :]
        for j in range(0, WIDE + 1, 2):
            if j + 1 < WIDE:
                right = w[j * 128:(j + 2) * 128, :]
            else:
                right = jnp.concatenate([w[j * 128:(j + 1) * 128, :], wtail[...]], axis=0)
            out = lax.dot_general(left, right, (((1,), (1,)), ((), ())), preferred_element_type=F32)
            for q in range(8):
                rows = out[q * 32:(q + 1) * 32]
                part[group * 8 + q, j * 2:(j + 1) * 2] = rows[:, :128].reshape(2, 16, 128)
                if j + 1 < WIDE:
                    part[group * 8 + q, (j + 1) * 2:(j + 2) * 2] = rows[:, 128:].reshape(2, 16, 128)
                else:
                    tail = rows[:, 128:].reshape(4, 8, 128)
                    packed = tail[0]
                    for i in range(1, 4):
                        packed = jnp.where(lane == i, tail[i], packed)
                    part[group * 8 + q, 2 * WIDE, :8] = packed

    def group_of(dy):
        for dx in (0, 1):
            for p in (0, 1):
                shared(dx, dy, p)
        product(dy)

    group_of(0)
    for p in (0, 1):
        for dy in (1, 3):
            arrived(1, dy, p)
            go(to_core(1, dy, p))
    group_of(1)
    act_step(3)
    for p in (0, 1):
        arrived(1, 2, p)
        go(to_core(1, 2, p))
    group_of(3)
    group_of(2)

    def owner_on(way, k):
        return (z + HALF - k) % Z if way == 0 else (z + HALF + k) % Z

    def mine_of(line, zz):
        place = owner_at((xl + line) % 2, zz)
        return part[place, :2 * WIDE], part[place, 2 * WIDE, :8]

    def sum_hop(way, k, line):
        return remote(out.at[way, k, line], ring.at[way, k, line], s_send.at[way, k, line], s_recv.at[way, k, line],
                      dl=1 if k == HALF - 1 and line == 1 else 0, dz=1 if way == 0 else Z - 1)

    def arrived_sum(way, k, line):
        sum_hop(way, k, line).wait_recv()
        return decode(ring[way, k, line, :2 * WIDE], ring[way, k, line, 2 * WIDE])

    def put(ref, main, rest):
        ref[:2 * WIDE] = main
        ref[2 * WIDE] = rest

    def sum_step(k):
        for line in (1, 0):
            for way in (0, 1):
                if k < FIRST[line][way]:
                    continue
                main, tail = mine_of(line, owner_on(way, k))
                if k > FIRST[line][way]:
                    more, rest = arrived_sum(way, k - 1, line)
                    main, tail = main + more, tail + rest
                put(out.at[way, k, line], *encode(main, tail))
                go(sum_hop(way, k, line))

    def weight_grad(start, width):
        cols = pl.ds(start, width)
        dw[:, cols] = lax.dot_general(
            act[...], og[:, cols], (((0,), (0,)), ((), ())),
            preferred_element_type=F32).astype(BF16)
        pltpu.make_async_copy(dw.at[:, cols], dw_hbm.at[:, cols], out_sem.at[start // 256]).start()

    swap = remote(last.at[0], last.at[1], l_send, l_recv, dl=1)
    for k in range(HALF):
        if "noS" not in FLAGS:
            sum_step(k)
        if k == 0:
            put(last.at[0], *encode(*mine_of(1, z)))
            go(swap)
        if k + 4 <= HALF + 1:
            act_step(k + 4)
        if "noDW" in FLAGS:
            continue
        if k == 6:
            for zz in range(Z):
                for p in (0, 1):
                    act_x(1, zz, p).wait_recv()

            @pl.loop(0, 2 * Z)
            def _(place):
                unpack(act_pk, place, 2, act, place * 32)

            weight_grad(0, 256)
        if k == 7:
            weight_grad(256, 256)
            weight_grad(512, 256)
            weight_grad(768, 160)

    main, tail = mine_of(0, z)
    swap.wait_recv()
    for more, rest in [decode(last[1, :2 * WIDE], last[1, 2 * WIDE])] + [
            arrived_sum(way, HALF - 1, line) for line in (0, 1) for way in (0, 1) if "noS" not in FLAGS]:
        main, tail = main + more, tail + rest
    for j in range(WIDE):
        din_ref[:, j * 128:(j + 1) * 128] = main[2 * j:2 * j + 2].reshape(32, 128).astype(BF16)
    for i in range(0, 4, 2):
        pair = [tail[:, 32 * (i + h):32 * (i + h + 1)] for h in (0, 1)]
        din_ref[8 * i:8 * i + 16, MAIN:] = jnp.concatenate(pair, axis=0).astype(BF16)
    if "noDW" not in FLAGS:
        for i, width in enumerate((256, 256, 256, 160)):
            cols = pl.ds(256 * i, width)
            pltpu.make_async_copy(dw.at[:, cols], dw_hbm.at[:, cols], out_sem.at[i]).wait()
    if "noDW" in FLAGS and "noC" not in FLAGS:
        for zz in range(Z):
            for p in (0, 1):
                act_x(1, zz, p).wait_recv()
    for copy in waits:
        copy.wait_send()


def hand_over(din_in, dw_in, din_out, dw_out):
    din_out[...] = din_in[...]
    dw_out[...] = dw_in[...]


def on_device(activations, out_grad, weight):
    model, hidden = weight.shape
    dma = pltpu.SemaphoreType.DMA
    din, dw = pl.pallas_call(
        kernel,
        out_shape=(jax.ShapeDtypeStruct(activations.shape, BF16), jax.ShapeDtypeStruct(weight.shape, BF16)),
        in_specs=[pl.BlockSpec(memory_space=pl.ANY)] * 3,
        out_specs=(pl.BlockSpec(memory_space=pltpu.VMEM), pl.BlockSpec(memory_space=pl.ANY)),
        scratch_shapes=[
            pltpu.VMEM((2 * Z * 32, model), BF16),
            pltpu.VMEM((2 * Z * 32, hidden), BF16),
            pltpu.VMEM((model, hidden), BF16),
            pltpu.VMEM((128, hidden), BF16),
            pltpu.VMEM((2 * Z, ACT, 16, 128), BF16),
            pltpu.VMEM((4 * Y, OG, 16, 128), BF16),
            pltpu.VMEM((2 * Z, SUM, 16, 128), F32),
            pltpu.VMEM((2, HALF, 2, SUM, 16, 128), BF16),
            pltpu.VMEM((2, HALF, 2, SUM, 16, 128), BF16),
            pltpu.VMEM((2, SUM, 16, 128), BF16),
            pltpu.VMEM((model, hidden), BF16),
            dma((3,)), dma((4,)),
            dma((2, Y, 2)), dma((2, Y, 2)),
            dma((2, Y, 2)), dma((2, Y, 2)),
            dma((Z, 2)), dma((Z, 2)),
            dma((2, HALF + 1, 2)), dma((2, HALF + 1, 2)),
            dma((2, HALF, 2)), dma((2, HALF, 2)),
            dma(()), dma(()),
        ],
        compiler_params=pltpu.CompilerParams(
            collective_id=0, has_side_effects=True, vmem_limit_bytes=60 << 20),
        name="backward",
    )(activations, out_grad, weight)
    return pl.pallas_call(
        hand_over,
        out_shape=(jax.ShapeDtypeStruct(din.shape, BF16), jax.ShapeDtypeStruct(dw.shape, BF16)),
        grid=(2,),
        in_specs=[pl.BlockSpec((16, model), lambda i: (i, 0)), pl.BlockSpec((model // 2, hidden), lambda i: (i, 0))],
        out_specs=[pl.BlockSpec((16, model), lambda i: (i, 0)), pl.BlockSpec((model // 2, hidden), lambda i: (i, 0))],
        name="outputs",
    )(din, dw)


def solution(mesh):
    return jax.shard_map(
        on_device,
        mesh=mesh,
        in_specs=(P("col", "row"), P("row", "col"), P("row", "col")),
        out_specs=(P("col", "row"), P("row", "col")),
        check_vma=False,
    )
```

time: 81.6 us -> 67.6 us (0.83)
  Pallas kernels: 75.1 us -> 65.7 us
  local copies, waits for them, and re-layouts: 4.39 us -> 0 us
    pallas_call x1, Pallas kernels: 75.1 us -> 63.1 us  [on_device(): pl.pallas_call(kernel, out_shape=(jax.ShapeDtypeStruct(activations.shape,...]
    unnamed x2 -> x0, local copies, waits for them, and re-layouts: 4.39 us -> none
    pallas_call x0 -> x1, Pallas kernels: none -> 2.56 us  [on_device(): pl.pallas_call(hand_over, out_shape=(jax.ShapeDtypeStruct(din.shape, BF16...]
where the time goes in v3:
time: 67.6 us; the launch traced here: 66.3 us
  Pallas kernels  65.7 us (97%)
    pallas_call x1, Pallas kernels, on_device(): pl.pallas_call(kernel, out_shape=(jax.ShapeDtypeStruct(activations.shape,...  63.1 us
    pallas_call x1, Pallas kernels, on_device(): pl.pallas_call(hand_over, out_shape=(jax.ShapeDtypeStruct(din.shape, BF16...  2.56 us

profile of v3, /device:TPU:24, one launch (start us, length us, event | category | flops | bytes accessed | tf_op | source)
XLA Modules:
  0.0 66.3 jit_solution(4695930142282439749)
XLA Ops:
  0.6 63.1 %backward.1 = (bf16[32,928]{1,0:T(8,128)(2,1)}, bf16[928,928]{1,0:T(8,128)(2,1)}) custom-call(bf16[32,928]{1,0:T(8,128)(2,1)} %act_hbm.1, bf16[64,928]{1,0:T(8,128)(2,1)} %og_hbm.1, bf16[928,928]{1,0:T(8,128)(2,1)} %w_hbm.1), custom_call_target="tpu_custom_call" | custom-call | tf_op jit(solution)/shard_map/backward/pallas_call | solution.py:357
  63.8 2.6 %outputs.1 = (bf16[32,928]{1,0:T(8,128)(2,1)}, bf16[928,928]{1,0:T(8,128)(2,1)}) custom-call(bf16[32,928]{1,0:T(8,128)(2,1)} %get-tuple-element.4.din_in, bf16[928,928]{1,0:T(8,128)(2,1)} %get-tuple-element.5.dw_in), custom_call_target="tpu_custom_call" | custom-call | tf_op jit(solution)/shard_map/outputs/pallas_call | solution.py:386

commit v4 on v3

--- a/solution.py
+++ b/solution.py
@@ -8,7 +8,6 @@
 MESH = pl.DeviceIdType.MESH
 F32 = jnp.float32
 BF16 = jnp.bfloat16
-FLAGS = set()
 Y, Z = 4, 16
 HALF = Z // 2
 WIDE = 7
@@ -115,8 +114,6 @@
 
     get_og.wait()
     pack(og, mine_og * 64, 4, og_pk, mine_og)
-    get_act.wait()
-    pack(act, mine_act * 32, 2, act_pk, mine_act)
     pl.semaphore_wait(barrier, len(near))
 
     def og_piece(dx, dy, dcore, p):
@@ -131,9 +128,9 @@
         ref = og_piece(dx, 0, 0, p)
         return remote(ref, ref, r_send.at[dx, dy, p], r_recv.at[dx, (Y - dy) % Y, p], dy=dy)
 
-    def over_x(p):
-        ref = og_piece(0, 2, 0, p)
-        return remote(ref, ref, r_send.at[1, 2, p], r_recv.at[1, 2, p], dx=1)
+    def over_x(dy):
+        ref = og_piece(0, dy, 0, 1)
+        return remote(ref, ref, r_send.at[1, dy, 1], r_recv.at[1, dy, 1], dx=1)
 
     def to_core(dx, dy, p):
         ref = og_piece(dx, dy, 0, p)
@@ -149,11 +146,11 @@
 
     for p in (0, 1):
         go(to_x(p))
-    for p in (0, 1):
+    go(to_y(0, 2, 1))
+    for p in (1, 0):
         for dy in (1, 3):
             go(to_y(0, dy, p))
-    for p in (0, 1):
-        go(to_y(0, 2, p))
+    go(to_y(0, 2, 0))
 
     def act_piece(line, zz, p):
         return act_pk.at[owner_at((xl + line) % 2, zz), pl.ds(ACT_CUT[p], ACT_CUT[p + 1] - ACT_CUT[p])]
@@ -172,8 +169,6 @@
     hops = (HALF, HALF - 1)
 
     def act_step(step):
-        if "noC" in FLAGS:
-            return
         for p in (0, 1):
             for way in (0, 1):
                 if 2 <= step <= hops[way] + 1:
@@ -185,10 +180,11 @@
                 if 2 <= step <= hops[way] + 1:
                     go(act_x(0, back(way, step - 1), p))
 
+    get_act.wait()
+    pack(act, mine_act * 32, 2, act_pk, mine_act)
     act_step(1)
-    if "noC" not in FLAGS:
-        for p in (0, 1):
-            go(act_x(0, z, p))
+    for p in (0, 1):
+        go(act_x(0, z, p))
     for p in (0, 1):
         go(to_core(0, 0, p))
 
@@ -196,30 +192,25 @@
     for i in range(4):
         wtail[32 * i:32 * (i + 1), :] = w[MAIN:, :]
 
-    for p in (0, 1):
-        arrived(1, 0, p)
-        for dy in (1, 3):
-            go(to_y(1, dy, p))
-        if p == 0:
-            go(to_y(1, 2, p))
+    arrived(1, 0, 0)
+    for dy in (1, 3, 2):
+        go(to_y(1, dy, 0))
+    for dy in (2, 1, 3):
+        arrived(0, dy, 1)
+        go(over_x(dy))
+    arrived(1, 0, 1)
+    for p in (0, 1):
         go(to_core(1, 0, p))
-    for p in (0, 1):
-        for dy in (1, 3):
-            arrived(0, dy, p)
+    for dy in (1, 3, 2):
+        arrived(0, dy, 0)
+        for p in (1, 0):
             go(to_core(0, dy, p))
-    for p in (1, 0):
-        arrived(0, 2, p)
-        if p == 1:
-            go(over_x(p))
-        go(to_core(0, 2, p))
     act_step(2)
 
     lane = lax.broadcasted_iota(jnp.int32, (8, 128), 1) // 32
 
     def product(dy):
         group = (y + dy) % Y
-        if "noP" in FLAGS:
-            return
         for i in range(4):
             unpack(og_pk, group * 4 + i, 4, og, (group * 4 + i) * 64)
         left = og[pl.ds(pl.multiple_of(group * 256, 256), 256), :]
@@ -279,17 +270,25 @@
         ref[:2 * WIDE] = main
         ref[2 * WIDE] = rest
 
+    def sum_send(way, k, line, main, tail):
+        put(out.at[way, k, line], *encode(main, tail))
+        go(sum_hop(way, k, line))
+
     def sum_step(k):
+        if k == 0:
+            for first in (0, 1):
+                for line in (1, 0):
+                    for way in (0, 1):
+                        if FIRST[line][way] == first:
+                            sum_send(way, first, line, *mine_of(line, owner_on(way, first)))
+            return
         for line in (1, 0):
             for way in (0, 1):
-                if k < FIRST[line][way]:
+                if k <= FIRST[line][way]:
                     continue
                 main, tail = mine_of(line, owner_on(way, k))
-                if k > FIRST[line][way]:
-                    more, rest = arrived_sum(way, k - 1, line)
-                    main, tail = main + more, tail + rest
-                put(out.at[way, k, line], *encode(main, tail))
-                go(sum_hop(way, k, line))
+                more, rest = arrived_sum(way, k - 1, line)
+                sum_send(way, k, line, main + more, tail + rest)
 
     def weight_grad(start, width):
         cols = pl.ds(start, width)
@@ -300,15 +299,12 @@
 
     swap = remote(last.at[0], last.at[1], l_send, l_recv, dl=1)
     for k in range(HALF):
-        if "noS" not in FLAGS:
-            sum_step(k)
+        sum_step(k)
         if k == 0:
             put(last.at[0], *encode(*mine_of(1, z)))
             go(swap)
         if k + 4 <= HALF + 1:
             act_step(k + 4)
-        if "noDW" in FLAGS:
-            continue
         if k == 6:
             for zz in range(Z):
                 for p in (0, 1):
@@ -327,28 +323,32 @@
     main, tail = mine_of(0, z)
     swap.wait_recv()
     for more, rest in [decode(last[1, :2 * WIDE], last[1, 2 * WIDE])] + [
-            arrived_sum(way, HALF - 1, line) for line in (0, 1) for way in (0, 1) if "noS" not in FLAGS]:
+            arrived_sum(way, HALF - 1, line) for line in (0, 1) for way in (0, 1)]:
         main, tail = main + more, tail + rest
     for j in range(WIDE):
         din_ref[:, j * 128:(j + 1) * 128] = main[2 * j:2 * j + 2].reshape(32, 128).astype(BF16)
     for i in range(0, 4, 2):
         pair = [tail[:, 32 * (i + h):32 * (i + h + 1)] for h in (0, 1)]
         din_ref[8 * i:8 * i + 16, MAIN:] = jnp.concatenate(pair, axis=0).astype(BF16)
-    if "noDW" not in FLAGS:
-        for i, width in enumerate((256, 256, 256, 160)):
-            cols = pl.ds(256 * i, width)
-            pltpu.make_async_copy(dw.at[:, cols], dw_hbm.at[:, cols], out_sem.at[i]).wait()
-    if "noDW" in FLAGS and "noC" not in FLAGS:
-        for zz in range(Z):
-            for p in (0, 1):
-                act_x(1, zz, p).wait_recv()
+    for i, width in enumerate((256, 256, 256, 160)):
+        cols = pl.ds(256 * i, width)
+        pltpu.make_async_copy(dw.at[:, cols], dw_hbm.at[:, cols], out_sem.at[i]).wait()
     for copy in waits:
         copy.wait_send()
 
 
-def hand_over(din_in, dw_in, din_out, dw_out):
-    din_out[...] = din_in[...]
-    dw_out[...] = dw_in[...]
+def hand_over(din_in, dw_in, din_out, dw_out, din, dw, sem_in, sem_out):
+    rows = [pl.ds(i, min(256, dw_in.shape[0] - i)) for i in range(0, dw_in.shape[0], 256)]
+    parts = [(dw_in.at[r], dw.at[r], dw_out.at[r]) for r in rows] + [(din_in, din, din_out)]
+    ins = [pltpu.make_async_copy(a, b, sem_in.at[i]) for i, (a, b, _) in enumerate(parts)]
+    outs = [pltpu.make_async_copy(b, c, sem_out.at[i]) for i, (_, b, c) in enumerate(parts)]
+    for copy in ins:
+        copy.start()
+    for got, put in zip(ins, outs):
+        got.wait()
+        put.start()
+    for put in outs:
+        put.wait()
 
 
 def on_device(activations, out_grad, weight):
@@ -386,9 +386,11 @@
     return pl.pallas_call(
         hand_over,
         out_shape=(jax.ShapeDtypeStruct(din.shape, BF16), jax.ShapeDtypeStruct(dw.shape, BF16)),
-        grid=(2,),
-        in_specs=[pl.BlockSpec((16, model), lambda i: (i, 0)), pl.BlockSpec((model // 2, hidden), lambda i: (i, 0))],
-        out_specs=[pl.BlockSpec((16, model), lambda i: (i, 0)), pl.BlockSpec((model // 2, hidden), lambda i: (i, 0))],
+        in_specs=[pl.BlockSpec(memory_space=pl.ANY)] * 2,
+        out_specs=[pl.BlockSpec(memory_space=pl.ANY)] * 2,
+        scratch_shapes=[pltpu.VMEM(din.shape, BF16), pltpu.VMEM(dw.shape, BF16),
+                        pltpu.SemaphoreType.DMA((5,)), pltpu.SemaphoreType.DMA((5,))],
+        compiler_params=pltpu.CompilerParams(vmem_limit_bytes=60 << 20),
         name="outputs",
     )(din, dw)
 

time: 67.6 us -> 67.7 us (level)
    pallas_call x1, Pallas kernels: 63.1 us -> 63.9 us  [on_device(): pl.pallas_call(kernel, out_shape=(jax.ShapeDtypeStruct(activations.shape,...]
where the time goes in v4:
time: 67.7 us; the launch traced here: 66.9 us
  Pallas kernels  66.3 us (98%)
    pallas_call x1, Pallas kernels, on_device(): pl.pallas_call(kernel, out_shape=(jax.ShapeDtypeStruct(activations.shape,...  63.9 us
    pallas_call x1, Pallas kernels, on_device(): pl.pallas_call(hand_over, out_shape=(jax.ShapeDtypeStruct(din.shape, BF16...  2.38 us

profile of v4, /device:TPU:24, one launch (start us, length us, event | category | flops | bytes accessed | tf_op | source)
XLA Modules:
  0.0 66.9 jit_solution(11036807656317135136)
XLA Ops:
  0.6 63.9 %backward.1 = (bf16[32,928]{1,0:T(8,128)(2,1)}, bf16[928,928]{1,0:T(8,128)(2,1)}) custom-call(bf16[32,928]{1,0:T(8,128)(2,1)} %act_hbm.1, bf16[64,928]{1,0:T(8,128)(2,1)} %og_hbm.1, bf16[928,928]{1,0:T(8,128)(2,1)} %w_hbm.1), custom_call_target="tpu_custom_call" | custom-call | tf_op jit(solution)/shard_map/backward/pallas_call | solution.py:357
  64.5 2.4 %outputs.1 = (bf16[32,928]{1,0:T(8,128)(2,1)}, bf16[928,928]{1,0:T(8,128)(2,1)}) custom-call(bf16[32,928]{1,0:T(8,128)(2,1)} %get-tuple-element.4.din_in, bf16[928,928]{1,0:T(8,128)(2,1)} %get-tuple-element.5.dw_in), custom_call_target="tpu_custom_call" | custom-call | tf_op jit(solution)/shard_map/outputs/pallas_call | solution.py:386
